TPU v7x, 32 devices: a whole 2x2x4 slice. The times are simulated.
32 devices in a mesh: energy: 8 (over y, x, core), chain: 4 (over z).
Axes of the slice: x: 2, y: 2, z: 4, core: 2. Of those that a mesh axis runs over, the one named last changes fastest.
Arguments:
- onsite: float32 [4, 2, 128, 128], P('chain'), may hold values from -0.5 to 0.5
- coupling: float32 [4, 2, 128, 128], P('chain'), may hold values from -0.3125 to 0.3125
- retained: int32 [4, 8192], P('chain'), may hold values from 0 to 16383
Outputs:
- polarization: float32 [2, 8, 4, 8192], P(None, None, 'chain', 'energy')
All inputs are finite; a program needn't handle non-finite values.
Results may differ from a plain program's by a relative error of at most 0.0003.
Values sent between devices are 32-bit elements; how exact they have to be, the bound alone decides.
A program may use at most 64 MiB of HBM per device.

v0:
```python
import math

import jax
import jax.numpy as jnp
from jax import lax
from jax.sharding import PartitionSpec as P

E_DEV = 1


broadening = 0.04


def shifted_2(value, axis, by):
    peers = lax.axis_size(axis)
    pairs = [(i, i + by) for i in range(peers) if 0 <= i + by < peers]
    return lax.ppermute(value, axis, pairs)


def product(left_part, right_part):
    return jnp.matmul(left_part, right_part, precision=lax.Precision.HIGHEST)


def represent(real_part, imag_part):
    upper_half = jnp.concatenate([real_part, -imag_part], axis=-1)
    lower_half = jnp.concatenate([imag_part, real_part], axis=-1)
    return jnp.concatenate([upper_half, lower_half], axis=-2)


def hermitian(raw_block):
    real_part = 0.5 * (raw_block[0] + raw_block[0].T)
    imag_part = 0.5 * (raw_block[1] - raw_block[1].T)
    return represent(real_part, imag_part)


def contact_term(coupler):
    orbitals = coupler.shape[0] // 2
    square = product(coupler, coupler.T)
    return represent(0.5 * square[orbitals:, :orbitals], -0.5 * square[:orbitals, :orbitals])


def split_parts(matrix, orbitals):
    return jnp.stack([matrix[:orbitals, :orbitals], matrix[orbitals:, :orbitals]])


def invert(matrix):
    normal = product(matrix.T, matrix)
    factor = jnp.linalg.cholesky(normal)
    first = jax.scipy.linalg.cho_solve((factor, True), matrix.T)
    remainder = jnp.eye(matrix.shape[0], dtype=jnp.float32) - product(matrix, first)
    return first + product(first, remainder)


def dft_tables(length):
    positions = jnp.arange(length, dtype=jnp.int32)
    phases = positions[:, None] * positions[None, :] % length
    angles = phases.astype(jnp.float32) * (2.0 * math.pi / length)
    return (jnp.cos(angles), jnp.sin(angles))


def correlate(left_real, left_imag, right_real, right_imag):
    cosine_table, sine_table = dft_tables(left_real.shape[0])
    turn_real = product(cosine_table, left_real) - product(sine_table, left_imag)
    turn_imag = product(cosine_table, left_imag) + product(sine_table, left_real)
    back_real = product(cosine_table, right_real) + product(sine_table, right_imag)
    back_imag = product(cosine_table, right_imag) - product(sine_table, right_real)
    prod_real = turn_real * back_real - turn_imag * back_imag
    prod_imag = turn_real * back_imag + turn_imag * back_real
    inverse_count = 1.0 / left_real.shape[0]
    out_real = (product(cosine_table, prod_real) - product(sine_table, prod_imag)) * inverse_count
    out_imag = (product(cosine_table, prod_imag) + product(sine_table, prod_real)) * inverse_count
    return (out_real, out_imag)


def spectra(received):
    energy_total = received.shape[0]
    column_count = received.shape[1] * received.shape[3]
    columns = [
        received[:, :, part_index, :].reshape(energy_total, column_count) for part_index in range(4)
    ]
    out_real, out_imag = correlate(columns[0], columns[1], columns[2], columns[3])
    return jnp.stack([out_real, out_imag]).reshape(
        2, energy_total, received.shape[1], received.shape[3]
    )


def shards(onsite, coupling, retained):
    orbitals = onsite.shape[-1]
    wide_width = 2 * orbitals
    blocks = onsite.shape[0]
    energy_count = E_DEV
    chains = lax.axis_size("chain")
    position = lax.axis_index("chain")
    groups = lax.axis_size("energy")
    all_energies = energy_count * groups
    offset = lax.axis_index("energy") * energy_count
    energies = (
        -2.0
        + 4.0
        * (offset + jnp.arange(energy_count, dtype=jnp.int32)).astype(jnp.float32)
        / all_energies
    )
    identity = jnp.eye(orbitals, dtype=jnp.float32)
    diagonal_blocks = jax.vmap(hermitian)(onsite)
    couplers = represent(coupling[:, 0], coupling[:, 1])
    at_end = (position == chains - 1).astype(jnp.float32)
    closing = contact_term(couplers[blocks - 1]) * at_end

    def forward(energy, incoming):
        sigma_block = represent(incoming[0], incoming[1])
        shifted = represent(energy * identity, broadening * identity)
        matrix = shifted - diagonal_blocks[0] - sigma_block
        matrix = matrix - closing
        inverse = invert(matrix)
        inverses = [inverse]
        sigma_block = product(product(couplers[0].T, inverse), couplers[0])
        return (jnp.stack(inverses), split_parts(sigma_block, orbitals))

    def backward(local_stack, incoming):
        following = represent(incoming[0], incoming[1])
        full_list = [None] * blocks
        for block_index in reversed(range(blocks)):
            inverse = local_stack[block_index]
            left_part = product(inverse, couplers[block_index])
            right_part = product(couplers[block_index].T, inverse)
            full_list[block_index] = inverse + product(product(left_part, following), right_part)
            following = full_list[block_index]
        return (jnp.stack(full_list), split_parts(following, orbitals))

    greens = jnp.zeros((energy_count, blocks, wide_width, wide_width), jnp.float32)
    full_blocks = jnp.zeros_like(greens)
    empty_all = jnp.zeros((energy_count, 2, orbitals, orbitals), jnp.float32)

    def forward_section(section_index, carried):
        greens_now, outgoing = carried
        incoming = shifted_2(outgoing, "chain", 1)

        def forward_active(received):
            return jax.vmap(forward)(energies, received)

        def forward_waiting(received):
            return (greens_now, outgoing)

        return lax.cond(position == section_index, forward_active, forward_waiting, incoming)

    greens, unused = lax.fori_loop(0, chains, forward_section, (greens, empty_all))

    def backward_section(section_index, carried):
        fulls_now, outgoing = carried
        incoming = shifted_2(outgoing, "chain", -1)

        def backward_active(received):
            return jax.vmap(backward)(greens, received)

        def backward_waiting(received):
            return (fulls_now, outgoing)

        return lax.cond(
            position == chains - 1 - section_index, backward_active, backward_waiting, incoming
        )

    full_blocks, unused = lax.fori_loop(0, chains, backward_section, (full_blocks, empty_all))
    real_flat = full_blocks[:, :, :orbitals, :orbitals].reshape(
        energy_count, blocks, orbitals * orbitals
    )
    imag_flat = full_blocks[:, :, orbitals:, :orbitals].reshape(
        energy_count, blocks, orbitals * orbitals
    )
    mirror = retained % orbitals * orbitals + retained // orbitals
    direct_index = retained[None]
    mirror_index = mirror[None]
    gathered = jnp.stack(
        [
            jnp.take_along_axis(real_flat, direct_index, axis=2),
            jnp.take_along_axis(imag_flat, direct_index, axis=2),
            jnp.take_along_axis(real_flat, mirror_index, axis=2),
            jnp.take_along_axis(imag_flat, mirror_index, axis=2),
        ],
        axis=2,
    )
    return spectra(lax.all_to_all(gathered, "energy", split_axis=3, concat_axis=0, tiled=True))


def solution(mesh):
    in_specs = (P("chain", None, None, None), P("chain", None, None, None), P("chain", None))
    out_specs = P(None, None, "chain", "energy")
    return jax.shard_map(shards, mesh=mesh, in_specs=in_specs, out_specs=out_specs, check_vma=False)
```

profile of v0, /device:TPU:0, one launch (start us, length us, event | category | flops | bytes accessed | tf_op | source)
XLA Modules:
  0.0 603.6 jit_solution(17661108384683918666)
XLA Ops:
  0.0 0.8 fusion.123
  0.8 0.9 slice_bitcast_fusion.23
  1.8 0.4 fusion.43
  2.2 1.0 compare_select_fusion.1
  3.3 0.9 slice_bitcast_fusion.25
  4.4 0.9 fusion.125
  5.4 0.7 broadcast.165.clone
  6.1 159.1 %while.35 = (s32[]{:T(128)}, f32[1,1,256,256]{3,2,1,0:T(8,128)}, f32[1,2,128,128]{3,2,1,0:T(8,128)S(1)}, s32[]{:T(128)}, f32[1]{0:T(128)}, /*index=5*/f32[1,256,...) while((s32[]{:T(128)}, f32[1,1,256,256]{3,2,1,0:T(8,128)}, ...), condition=%wide.region_7.8_spmd.clone.clone, body=%wide.region_0.7_spmd.clone.clone.sunk | while | flops 1360756992 | bytes 12716502 | solution.py:146
  6.2 4.9 collective-permute-start.1
  11.1 2.7 collective-permute-done.1
  13.8 66.7 %conditional.7 = ((f32[1,1,256,256]{3,2,1,0:T(8,128)}, f32[1,2,128,128]{3,2,1,0:T(8,128)S(1)})) conditional(s32[]{:T(128)} %convert_element_type.94, (f32[1,1,256,256]{3,2,1,0:T(8,128)}, f32[1,2,128,128]{3,2,1,0:T(8,128)S(1)}) %tuple.114, (f32[1]{0:T(128)}, f32[128,128]{0,1:T(8,128)S(1)}, f32[128,128]{0,1:T(8,128)S(1)}, f32[128,128]{0,1:T(8,128)S(1)}, ...), branch_computations={%region_1.0_spmd, %region_2.6_spmd} | conditional | flops 1360724224 | bytes 11864299 | solution.py:144
  14.1 0.4 fusion.27
  14.7 11.7 %custom-call.16 = f32[1,128,128]{2,1,0:T(8,128)S(1)} custom-call(f32[1,128,128]{2,1,0:T(8,128)S(1)} %cholesky.45), custom_call_target="Cholesky" | custom-call | tf_op jit(solution)/shard_map/while/body/eval_jaxpr/cond/branch_1_fun/vmap(jit(cholesky))/cholesky | solution.py:48
  26.4 0.7 compare_reduce_fusion.1
  27.1 9.8 %custom-call.17 = f32[1,1,128,128]{2,3,1,0:T(8,128)S(1)} custom-call(f32[1,1,128,128]{3,2,1,0:T(8,128)S(1)} %get-tuple-element.432), custom_call_target="InvertDiagBlocksLowerTriangular" | custom-call | tf_op jit(solution)/shard_map/while/body/eval_jaxpr/cond/branch_1_fun/vmap(jit(cholesky))/cholesky | solution.py:48
  37.5 11.7 %custom-call.18 = f32[1,128,128]{2,1,0:T(8,128)S(1)} custom-call(f32[1,128,128]{2,1,0:T(8,128)S(1)} %fusion.19), custom_call_target="Cholesky" | custom-call | tf_op jit(solution)/shard_map/while/body/eval_jaxpr/cond/branch_1_fun/vmap(jit(cholesky))/cholesky | solution.py:48
  49.2 0.6 compare_reduce_fusion
  51.1 4.1 while.33
  51.2 0.7 fusion.148
  51.8 1.3 bitcast_dynamic-update-slice_fusion.3
  53.2 0.7 fusion.148
  53.9 1.3 bitcast_dynamic-update-slice_fusion.3
  55.2 19.7 %custom-call.19 = f32[1,2,128,128]{2,3,1,0:T(8,128)S(1)} custom-call(f32[1,2,128,128]{3,2,1,0:T(8,128)S(1)} %bitcast.264), custom_call_target="InvertDiagBlocksLowerTriangular" | custom-call | tf_op jit(solution)/shard_map/while/body/eval_jaxpr/cond/branch_1_fun/vmap(jit(_cho_solve))/triangular_solve | solution.py:49
  76.7 0.6 convolution_subtract_fusion
  77.3 1.1 convolution_add_fusion.1
  78.4 1.5 fusion.24
  79.9 0.6 convolution_bitcast_fusion
  80.7 1.3 collective-permute-start.1
  82.0 2.5 collective-permute-done.1
  84.6 71.1 %collective-permute-start.1 = (f32[1,2,128,128]{2,3,1,0:T(8,128)S(1)}, f32[1,2,128,128]{2,3,1,0:T(8,128)S(1)}, u32[]{:S(2)}, u32[]{:S(2)}) collective-permute-start(f32[1,2,128,128]{2,3,1,0:T(8,128)S(1)} %copy.33), channel_id=1, source_target_pairs={{0,1},{1,2},{2,3},{4,5},{5,6},{6,7},{8,9},{9,10},{10,11},{12,13},{... | collective-permute-start | bytes 393224 | tf_op jit(solution)/shard_map/while/body/eval_jaxpr/ppermute | solution.py:17
  155.7 2.5 collective-permute-done.1
  158.3 4.4 collective-permute-start.1
  162.7 2.5 collective-permute-done.1
  165.2 0.7 broadcast.165
  165.9 178.9 %while.34 = (s32[]{:T(128)}, f32[1,1,256,256]{3,2,1,0:T(8,128)}, f32[1,2,128,128]{3,2,1,0:T(8,128)S(1)}, s32[]{:T(128)}, f32[1,1,256,256]{3,2,1,0:T(8,128)}, /*i...) while((s32[]{:T(128)}, f32[1,1,256,256]{3,2,1,0:T(8,128)}, f32[1,2,128,128]{3,2,1,0:T(8,128)S(1)}, ...), condition=%wide.region_11.12_spmd, body=%wide.region_8.11_spmd.sunk | while | flops 805617664 | bytes 4784343 | solution.py:162
  165.9 1.3 collective-permute-start
  167.2 70.3 %collective-permute-done = f32[1,2,128,128]{3,2,1,0:T(8,128)S(1)} collective-permute-done((f32[1,2,128,128]{3,2,1,0:T(8,128)S(1)}, f32[1,2,128,128]{3,2,1,0:T(8,128)S(1)}, u32[]{:S(2)}, u32[]{:S(2)}) %collective-permute-start) | collective-permute-done | bytes 131104 | tf_op jit(solution)/shard_map/while/body/eval_jaxpr/ppermute | solution.py:17
  237.5 1.3 collective-permute-start
  238.8 6.0 collective-permute-done
  244.8 1.3 collective-permute-start
  246.1 69.9 %collective-permute-done = f32[1,2,128,128]{3,2,1,0:T(8,128)S(1)} collective-permute-done((f32[1,2,128,128]{3,2,1,0:T(8,128)S(1)}, f32[1,2,128,128]{3,2,1,0:T(8,128)S(1)}, u32[]{:S(2)}, u32[]{:S(2)}) %collective-permute-start) | collective-permute-done | bytes 131104 | tf_op jit(solution)/shard_map/while/body/eval_jaxpr/ppermute | solution.py:17
  316.0 1.3 collective-permute-start
  317.3 21.3 %collective-permute-done = f32[1,2,128,128]{3,2,1,0:T(8,128)S(1)} collective-permute-done((f32[1,2,128,128]{3,2,1,0:T(8,128)S(1)}, f32[1,2,128,128]{3,2,1,0:T(8,128)S(1)}, u32[]{:S(2)}, u32[]{:S(2)}) %collective-permute-start) | collective-permute-done | bytes 131104 | tf_op jit(solution)/shard_map/while/body/eval_jaxpr/ppermute | solution.py:17
  338.5 6.2 %conditional.6 = ((f32[1,1,256,256]{3,2,1,0:T(8,128)}, f32[1,2,128,128]{3,2,1,0:T(8,128)S(1)})) conditional(s32[]{:T(128)} %convert_element_type.92, (f32[1,1,256,256]{3,2,1,0:T(8,128)}, f32[1,2,128,128]{3,2,1,0:T(8,128)S(1)}) %tuple.111, (f32[1,1,256,256]{3,2,1,0:T(8,128)}, f32[1,256,256]{2,1,0:T(8,128)S(1)}, ...), branch_computations={%region_9.9_spmd, %region_10.10_spmd} | conditional | flops 805617664 | bytes 4259864 | solution.py:158
  338.5 1.5 fusion.9
  340.1 1.3 fusion.11
  341.4 0.4 fusion.2
  341.8 2.0 convolution_add_fusion
  343.9 0.9 slice_bitcast_fusion.1
  344.8 0.9 slice_bitcast_fusion.22
  345.7 45.5 %gather_fusion.2 = f32[8192]{0:T(1024)S(1)} fusion(f32[16384]{0:T(1024)S(1)} %get-tuple-element.437, s32[8192]{0:T(1024)S(1)} %broadcast_clamp_fusion), kind=kCustom, calls=%fused_computation.2.clone | custom fusion | bytes 98304 | tf_op jit(solution)/shard_map/jit(take_along_axis)/gather | solution.py:176
  391.2 45.5 %gather_fusion = f32[8192]{0:T(1024)S(1)} fusion(f32[16384]{0:T(1024)S(1)} %get-tuple-element.437, s32[8192]{0:T(1024)S(1)} %broadcast_clamp_fusion.1), kind=kCustom, calls=%fused_computation.clone | custom fusion | bytes 98304 | tf_op jit(solution)/shard_map/jit(take_along_axis)/gather | solution.py:174
  436.7 45.5 %gather_fusion.1 = f32[8192]{0:T(1024)S(1)} fusion(f32[16384]{0:T(1024)S(1)} %get-tuple-element.438, s32[8192]{0:T(1024)S(1)} %broadcast_clamp_fusion.1), kind=kCustom, calls=%fused_computation.1.clone | custom fusion | bytes 98304 | tf_op jit(solution)/shard_map/jit(take_along_axis)/gather | solution.py:175
  482.3 45.5 %gather_fusion.3 = f32[8192]{0:T(1024)S(1)} fusion(f32[16384]{0:T(1024)S(1)} %get-tuple-element.438, s32[8192]{0:T(1024)S(1)} %broadcast_clamp_fusion), kind=kCustom, calls=%fused_computation.3.clone | custom fusion | bytes 98304 | tf_op jit(solution)/shard_map/jit(take_along_axis)/gather | solution.py:177
  527.8 0.4 select_bitcast_fusion.4
  528.4 6.4 %copy.27 = f32[1,1,4,8192]{2,1,0,3:T(1,128)} copy(f32[1,1,4,8192]{3,2,1,0:T(4,128)S(1)} %pad_maximum_fusion) | data formatting | bytes 262144 | tf_op jit(solution)/shard_map/stack | solution.py:172
  534.7 0.5 broadcast.229
  535.2 38.4 %reduce.18 = f32[8192,4]{1,0:T(8,128)} reduce(f32[8192,1,1,4]{3,2,1,0:T(1,128)} %bitcast.248, f32[]{:T(128)} %broadcast.229), dimensions={1,2}, to_apply=%bitcast.209.reduce_sub_computation | reduce | bytes 262148
  573.6 5.0 reshape.356
  578.7 9.1 %all_to_all.18 = f32[8,1,4096]{2,1,0:T(1,128)S(1)} all-to-all(f32[8,1,4096]{2,1,0:T(1,128)S(1)} %reshape.356), channel_id=1, replica_groups=mesh['energy'=8,'chain'=4] {'energy'}, dimensions={0} | all-to-all | bytes 262144 | tf_op jit(solution)/shard_map/all_to_all | solution.py:181
  587.8 1.0 reduce.19
  588.7 8.7 %reshape.357 = f32[8192,1,1,4]{3,2,1,0:T(1,128)} reshape(f32[8,4096]{1,0:T(8,128)S(1)} %reduce.19) | data formatting | bytes 262144
  597.4 2.9 copy.31
  602.9 0.7 copy.29
  (70 shorter events, 6.1 us)
Async XLA Ops:
  6.2 7.7 %collective-permute-start.1 = (f32[1,2,128,128]{2,3,1,0:T(8,128)S(1)}, f32[1,2,128,128]{2,3,1,0:T(8,128)S(1)}, u32[]{:S(2)}, u32[]{:S(2)}) collective-permute-start(f32[1,2,128,128]{2,3,1,0:T(8,128)S(1)} %copy.33), channel_id=1, source_target_pairs={{0,1},{1,2},{2,3},{4,5},{5,6},{6,7},{8,9},{9,10},{10,11},{12,13},{... | collective-permute-start | bytes 393224 | tf_op jit(solution)/shard_map/while/body/eval_jaxpr/ppermute | solution.py:17
  80.7 3.8 collective-permute-start.1
  84.6 73.6 %collective-permute-start.1 = (f32[1,2,128,128]{2,3,1,0:T(8,128)S(1)}, f32[1,2,128,128]{2,3,1,0:T(8,128)S(1)}, u32[]{:S(2)}, u32[]{:S(2)}) collective-permute-start(f32[1,2,128,128]{2,3,1,0:T(8,128)S(1)} %copy.33), channel_id=1, source_target_pairs={{0,1},{1,2},{2,3},{4,5},{5,6},{6,7},{8,9},{9,10},{10,11},{12,13},{... | collective-permute-start | bytes 393224 | tf_op jit(solution)/shard_map/while/body/eval_jaxpr/ppermute | solution.py:17
  158.3 6.9 %collective-permute-start.1 = (f32[1,2,128,128]{2,3,1,0:T(8,128)S(1)}, f32[1,2,128,128]{2,3,1,0:T(8,128)S(1)}, u32[]{:S(2)}, u32[]{:S(2)}) collective-permute-start(f32[1,2,128,128]{2,3,1,0:T(8,128)S(1)} %copy.33), channel_id=1, source_target_pairs={{0,1},{1,2},{2,3},{4,5},{5,6},{6,7},{8,9},{9,10},{10,11},{12,13},{... | collective-permute-start | bytes 393224 | tf_op jit(solution)/shard_map/while/body/eval_jaxpr/ppermute | solution.py:17
  165.9 71.6 %collective-permute-start = (f32[1,2,128,128]{3,2,1,0:T(8,128)S(1)}, f32[1,2,128,128]{3,2,1,0:T(8,128)S(1)}, u32[]{:S(2)}, u32[]{:S(2)}) collective-permute-start(f32[1,2,128,128]{3,2,1,0:T(8,128)S(1)} %get-tuple-element.638), channel_id=1, source_target_pairs={{1,0},{2,1},{3,2},{5,4},{6,5},{7,6},{9,8},{10,9},{11,10},{13,12},{... | collective-permute-start | bytes 393224 | tf_op jit(solution)/shard_map/while/body/eval_jaxpr/ppermute | solution.py:17
  237.5 7.3 %collective-permute-start = (f32[1,2,128,128]{3,2,1,0:T(8,128)S(1)}, f32[1,2,128,128]{3,2,1,0:T(8,128)S(1)}, u32[]{:S(2)}, u32[]{:S(2)}) collective-permute-start(f32[1,2,128,128]{3,2,1,0:T(8,128)S(1)} %get-tuple-element.638), channel_id=1, source_target_pairs={{1,0},{2,1},{3,2},{5,4},{6,5},{7,6},{9,8},{10,9},{11,10},{13,12},{... | collective-permute-start | bytes 393224 | tf_op jit(solution)/shard_map/while/body/eval_jaxpr/ppermute | solution.py:17
  244.8 71.2 %collective-permute-start = (f32[1,2,128,128]{3,2,1,0:T(8,128)S(1)}, f32[1,2,128,128]{3,2,1,0:T(8,128)S(1)}, u32[]{:S(2)}, u32[]{:S(2)}) collective-permute-start(f32[1,2,128,128]{3,2,1,0:T(8,128)S(1)} %get-tuple-element.638), channel_id=1, source_target_pairs={{1,0},{2,1},{3,2},{5,4},{6,5},{7,6},{9,8},{10,9},{11,10},{13,12},{... | collective-permute-start | bytes 393224 | tf_op jit(solution)/shard_map/while/body/eval_jaxpr/ppermute | solution.py:17
  316.0 22.6 %collective-permute-start = (f32[1,2,128,128]{3,2,1,0:T(8,128)S(1)}, f32[1,2,128,128]{3,2,1,0:T(8,128)S(1)}, u32[]{:S(2)}, u32[]{:S(2)}) collective-permute-start(f32[1,2,128,128]{3,2,1,0:T(8,128)S(1)} %get-tuple-element.638), channel_id=1, source_target_pairs={{1,0},{2,1},{3,2},{5,4},{6,5},{7,6},{9,8},{10,9},{11,10},{13,12},{... | collective-permute-start | bytes 393224 | tf_op jit(solution)/shard_map/while/body/eval_jaxpr/ppermute | solution.py:17
  482.3 45.6 %copy-start = (s32[1,8192]{1,0:T(1,128)S(1)}, s32[1,8192]{1,0:T(1,128)}, u32[]{:S(2)}) copy-start(s32[1,8192]{1,0:T(1,128)} %param.15) | copy-start | bytes 98308
where the time goes:
time: 605 us; the launch traced here: 604 us
  local copies, waits for them, and re-layouts  216 us (36%)
  waiting for transfers between devices  178 us (29%)
  other arithmetic  97.3 us (16%)
  starting transfers between devices  86.8 us (14%)
  matrix products  14.7 us (2%)
  blocking collectives  9.09 us (2%)
    ppermute x8, waiting for transfers between devices, shifted_2(): return lax.ppermute(value, axis, pairs)  178 us
    ppermute x8, starting transfers between devices, shifted_2(): return lax.ppermute(value, axis, pairs)  86.8 us
    gather x1, local copies, waits for them, and re-layouts, shards(): jnp.take_along_axis(real_flat, direct_index, axis=2)  45.5 us
    gather x1, local copies, waits for them, and re-layouts, shards(): jnp.take_along_axis(imag_flat, direct_index, axis=2)  45.5 us
    gather x1, local copies, waits for them, and re-layouts, shards(): jnp.take_along_axis(real_flat, mirror_index, axis=2)  45.5 us
    gather x1, local copies, waits for them, and re-layouts, shards(): jnp.take_along_axis(imag_flat, mirror_index, axis=2)  45.5 us
    unnamed x1, other arithmetic  38.4 us
    another operation x7, other arithmetic, invert(): factor = jnp.linalg.cholesky(normal)  34.7 us
  transfers between devices with their start and end apart: 8, of which 8 were waited for; matrix products, arithmetic and copies ran while one was open for 0% of the time, Pallas kernels for 0%

commit v1 on v0

v1 whole, which is shorter than its diff:
```python
import functools

import jax
import jax.numpy as jnp
from jax import lax
from jax.experimental import pallas as pl
from jax.experimental.pallas import tpu as pltpu
from jax.sharding import PartitionSpec as P

MESH = pl.DeviceIdType.MESH
PANEL = 8
BROADENING = 0.04


def product(left, right):
    wide = jnp.concatenate(left, axis=1)
    real, imag = right
    tall = jnp.concatenate(
        [jnp.concatenate([real, imag], axis=1), jnp.concatenate([-imag, real], axis=1)], axis=0
    )
    both = jnp.dot(
        wide, tall, precision=lax.Precision.HIGHEST, preferred_element_type=jnp.float32
    )
    size = real.shape[1]
    return both[:, :size], both[:, size:]


def adjoint(value):
    return value[0].T, -value[1].T


def load(ref):
    return ref[0], ref[1]


def store(ref, value):
    ref[0] = value[0]
    ref[1] = value[1]


def across(value, column):
    return jnp.broadcast_to(value[:, column : column + 1], value.shape)


def down(value, row):
    return jnp.broadcast_to(value[row : row + 1, :], value.shape)


def pivot_inverse(real, imag):
    rows = lax.broadcasted_iota(jnp.int32, real.shape, 0)
    cols_r = [across(real, c) for c in range(PANEL)]
    cols_i = [across(imag, c) for c in range(PANEL)]
    for k in range(PANEL):
        pivot_r, pivot_i = down(cols_r[k], k), down(cols_i[k], k)
        scale = 1.0 / (pivot_r * pivot_r + pivot_i * pivot_i)
        inv_r, inv_i = pivot_r * scale, -pivot_i * scale
        here = rows == k
        factor_r = jnp.where(here, -1.0, cols_r[k])
        factor_i = jnp.where(here, 0.0, cols_i[k])
        f_r = factor_r * inv_r - factor_i * inv_i
        f_i = factor_r * inv_i + factor_i * inv_r
        for c in range(PANEL):
            if c == k:
                continue
            m_r, m_i = down(cols_r[c], k), down(cols_i[c], k)
            cols_r[c] = jnp.where(here, 0.0, cols_r[c]) - (f_r * m_r - f_i * m_i)
            cols_i[c] = jnp.where(here, 0.0, cols_i[c]) - (f_r * m_i + f_i * m_r)
        cols_r[k], cols_i[k] = -f_r, -f_i
    return tuple(cols_r) + tuple(cols_i)


def invert(ref):
    size = ref.shape[-1]
    count = size // PANEL
    shape = (PANEL, size)
    lanes = lax.broadcasted_iota(jnp.int32, shape, 1)
    rows = lax.broadcasted_iota(jnp.int32, shape, 0)
    low = lanes < PANEL
    unit = (lanes == rows).astype(jnp.float32)

    def turn(value):
        return pltpu.roll(value, size - PANEL, 1)

    def step(s, pivot):
        p_r, p_i = pivot[:PANEL], pivot[PANEL:]
        here = pl.ds(pl.multiple_of(s * PANEL, PANEL), PANEL)
        a_r = jnp.where(low, unit, ref[0, here, :])
        a_i = jnp.where(low, 0.0, ref[1, here, :])
        r_r, r_i = jnp.zeros(shape, jnp.float32), jnp.zeros(shape, jnp.float32)
        for c in range(PANEL):
            b_r, b_i = down(a_r, c), down(a_i, c)
            r_r = r_r + (p_r[c] * b_r - p_i[c] * b_i)
            r_i = r_i + (p_r[c] * b_i + p_i[c] * b_r)
        rb_r = [down(r_r, c) for c in range(PANEL)]
        rb_i = [down(r_i, c) for c in range(PANEL)]

        def updated(at):
            x_r, x_i = ref[0, at, :], ref[1, at, :]
            y_r, y_i = jnp.where(low, 0.0, x_r), jnp.where(low, 0.0, x_i)
            for c in range(PANEL):
                c_r, c_i = across(x_r, c), across(x_i, c)
                y_r = y_r - (c_r * rb_r[c] - c_i * rb_i[c])
                y_i = y_i - (c_r * rb_i[c] + c_i * rb_r[c])
            return turn(y_r), turn(y_i)

        following = lax.rem(s + 1, count)
        ahead = updated(pl.ds(pl.multiple_of(following * PANEL, PANEL), PANEL))
        later = pivot_inverse(*ahead)
        for i in range(count):
            at = pl.ds(i * PANEL, PANEL)
            z_r, z_i = updated(at)
            ref[0, at, :] = z_r
            ref[1, at, :] = z_i
        ref[0, here, :] = turn(r_r)
        ref[1, here, :] = turn(r_i)
        return later

    first = pivot_inverse(ref[0, pl.ds(0, PANEL), :], ref[1, pl.ds(0, PANEL), :])
    lax.fori_loop(0, count, step, first)


def kernel(
    groups, chains, onsite, coupling, retained, out,
    base, work, toward, left, prev, sigma_in, green_in, sigma_out, picked, table, received,
    u_send, u_recv, s_send, s_recv, g_send, g_recv, a_send, a_recv,
):
    size = onsite.shape[-1]
    me = lax.axis_index("energy")
    pos = lax.axis_index("chain")
    half = chains // 2
    in_left = pos < half
    depth = jnp.where(in_left, pos, chains - 1 - pos)
    inner = jnp.where(in_left, pos + 1, pos - 1)
    outer = jnp.where(in_left, pos - 1, pos + 1)
    middle = depth == half - 1
    at_edge = depth == 0

    barrier = pltpu.get_barrier_semaphore()

    def greet(energy, chain):
        pl.semaphore_signal(barrier, inc=1, device_id=(energy, chain), device_id_type=MESH)

    for t in range(1, groups):
        greet(lax.rem(me + t, groups), pos)
    greet(me, inner)

    @pl.when(jnp.logical_not(at_edge))
    def _():
        greet(me, outer)

    def copy(src, dst, send, recv, energy, chain):
        return pltpu.make_async_remote_copy(
            src_ref=src, dst_ref=dst, send_sem=send, recv_sem=recv,
            device_id=(energy, chain), device_id_type=MESH,
        )

    coupling_copy = copy(coupling, prev, u_send, u_recv, me, lax.rem(pos + 1, chains))
    slot = jnp.where(middle, 1, 0)
    sigma_copy = copy(sigma_out, sigma_in.at[slot], s_send, s_recv.at[slot], me, inner)
    green_copy = copy(work, green_in, g_send, g_recv, me, jnp.clip(outer, 0, chains - 1))

    def sigma_arrival(which):
        copy(sigma_out, sigma_in.at[which], s_send, s_recv.at[which], me, inner).wait_recv()

    diagonal = (
        lax.broadcasted_iota(jnp.int32, (size, size), 0)
        == lax.broadcasted_iota(jnp.int32, (size, size), 1)
    ).astype(jnp.float32)
    energy = -2.0 + 4.0 * me.astype(jnp.float32) / groups
    base[0] = energy * diagonal - 0.5 * (onsite[0] + onsite[0].T)
    base[1] = BROADENING * diagonal - 0.5 * (onsite[1] - onsite[1].T)

    @pl.when(pos == chains - 1)
    def _():
        coupler = load(coupling)
        square = product(coupler, adjoint(coupler))
        base[0] = base[0] - 0.5 * square[1]
        base[1] = base[1] + 0.5 * square[0]

    pl.semaphore_wait(barrier, groups + jnp.where(at_edge, 0, 1))

    sends_coupling = jnp.logical_and(pos >= half - 1, pos < chains - 1)

    @pl.when(sends_coupling)
    def _():
        coupling_copy.start()

    @pl.when(jnp.logical_not(at_edge))
    def _():
        sigma_arrival(0)
        base[...] = base[...] - sigma_in[0]

    work[...] = base[...]
    invert(work)

    @pl.when(in_left)
    def _():
        toward[...] = coupling[...]

    @pl.when(jnp.logical_not(in_left))
    def _():
        coupling_copy.wait_recv()
        store(toward, adjoint(load(prev)))

    store(left, product(load(work), load(toward)))
    store(sigma_out, product(adjoint(load(toward)), load(left)))
    sigma_copy.start()

    @pl.when(middle)
    def _():
        sigma_arrival(1)
        work[...] = base[...] - sigma_in[1]
        invert(work)

    @pl.when(jnp.logical_not(middle))
    def _():
        right = product(adjoint(load(toward)), load(work))
        green_copy.wait_recv()
        change = product(product(load(left), load(green_in)), right)
        work[0] = work[0] + change[0]
        work[1] = work[1] + change[1]

    @pl.when(jnp.logical_not(at_edge))
    def _():
        green_copy.start()

    full = load(work)
    planes = jnp.concatenate([full[0], full[1], full[0].T, full[1].T], axis=0)
    high = planes.astype(jnp.bfloat16)
    low = (planes - high.astype(jnp.float32)).astype(jnp.bfloat16)
    table[...] = jnp.concatenate([high, low], axis=1)
    columns = retained.shape[-1]
    across_rows = columns // 128

    def pick(group, target, place):
        chosen = retained[group]
        spot = lax.broadcasted_iota(jnp.int32, (size, columns), 0)
        hot = (spot == chosen % size).astype(jnp.float32).astype(jnp.bfloat16)
        keep = spot == chosen // size
        rows = jnp.dot(
            table[...], jnp.concatenate([hot, hot], axis=0), preferred_element_type=jnp.float32
        )
        for p in range(4):
            part = jnp.where(keep, rows[p * size : (p + 1) * size], 0.0)
            line = jnp.sum(part, axis=0, keepdims=True)
            for r in range(across_rows):
                target[place, p, r : r + 1, :] = line[:, r * 128 : (r + 1) * 128]

    def exchange(t):
        peer = lax.rem(me + t, groups)
        return copy(
            picked.at[peer], received.at[me], a_send.at[peer], a_recv.at[me], peer, pos
        )

    def send_step(t, carry):
        peer = lax.rem(me + t, groups)
        pick(peer, picked, peer)
        exchange(t).start()
        return carry

    lax.fori_loop(1, groups, send_step, 0)
    pick(me, received, me)

    def arrive_step(t, carry):
        source = lax.rem(me + t, groups)
        copy(
            picked.at[source], received.at[source], a_send.at[source], a_recv.at[source],
            source, pos,
        ).wait_recv()
        return carry

    lax.fori_loop(1, groups, arrive_step, 0)

    def shift_step(w, carry):
        real = jnp.zeros(out.shape[2:], jnp.float32)
        imag = jnp.zeros(out.shape[2:], jnp.float32)
        for n in range(groups):
            other = lax.rem(w + n, groups)
            a_r, a_i = received[n, 0], received[n, 1]
            b_r, b_i = received[other, 2], received[other, 3]
            real = real + (a_r * b_r - a_i * b_i)
            imag = imag + (a_r * b_i + a_i * b_r)
        out[0, w] = real
        out[1, w] = imag
        return carry

    lax.fori_loop(0, groups, shift_step, 0)

    sigma_copy.wait_send()

    @pl.when(sends_coupling)
    def _():
        coupling_copy.wait_send()

    @pl.when(jnp.logical_not(at_edge))
    def _():
        green_copy.wait_send()

    def leave_step(t, carry):
        exchange(t).wait_send()
        return carry

    lax.fori_loop(1, groups, leave_step, 0)


def shards(onsite, coupling, retained):
    size = onsite.shape[-1]
    groups = lax.axis_size("energy")
    chains = lax.axis_size("chain")
    columns = retained.shape[-1] // groups
    block = pltpu.VMEM((2, size, size), jnp.float32)
    picks = pltpu.VMEM((groups, 4, columns // 128, 128), jnp.float32)
    dma = pltpu.SemaphoreType.DMA
    result = pl.pallas_call(
        functools.partial(kernel, groups, chains),
        out_shape=jax.ShapeDtypeStruct((2, groups, columns // 128, 128), jnp.float32),
        in_specs=[pl.BlockSpec(memory_space=pltpu.VMEM)] * 3,
        out_specs=pl.BlockSpec(memory_space=pltpu.VMEM),
        scratch_shapes=[
            block, block, block, block, block,
            pltpu.VMEM((2, 2, size, size), jnp.float32), block, block,
            picks,
            pltpu.VMEM((4 * size, 2 * size), jnp.bfloat16),
            picks,
            dma(()), dma(()), dma(()), dma((2,)), dma(()), dma(()),
            dma((groups,)), dma((groups,)),
        ],
        compiler_params=pltpu.CompilerParams(
            collective_id=0, has_side_effects=True, vmem_limit_bytes=32 * 1024 * 1024
        ),
    )(onsite[0], coupling[0], retained.reshape(groups, 1, columns))
    return result.reshape(2, groups, 1, columns)


def solution(mesh):
    in_specs = (P("chain", None, None, None), P("chain", None, None, None), P("chain", None))
    out_specs = P(None, None, "chain", "energy")
    return jax.shard_map(shards, mesh=mesh, in_specs=in_specs, out_specs=out_specs, check_vma=False)
```

time: 605 us -> 102 us (0.17)
  local copies, waits for them, and re-layouts: 216 us -> 3.2 us
  waiting for transfers between devices: 178 us -> 0 us
  Pallas kernels: 0 us -> 98.6 us
  other arithmetic: 97.3 us -> 0 us
  starting transfers between devices: 86.8 us -> 0 us
  matrix products: 14.7 us -> 0 us
  blocking collectives: 9.09 us -> 0 us
    gather x4 -> x0, local copies, waits for them, and re-layouts: 182 us -> none  [the longest x1 45.5 us: shards(): jnp.take_along_axis(real_flat, direct_index, axis=2)]
    ppermute x8 -> x0, waiting for transfers between devices: 178 us -> none  [shifted_2(): return lax.ppermute(value, axis, pairs)]
    pallas_call x0 -> x1, Pallas kernels: none -> 98.6 us  [shards(): pl.pallas_call(functools.partial(kernel, groups, chains), out_shape=jax.S...]
    ppermute x8 -> x0, starting transfers between devices: 86.8 us -> none  [shifted_2(): return lax.ppermute(value, axis, pairs)]
    another operation x12 -> x0, other arithmetic: 54.9 us -> none  [the longest x7 34.7 us: invert(): factor = jnp.linalg.cholesky(normal)]
    unnamed x1 -> x0, other arithmetic: 38.4 us -> none
    another operation x15 -> x0, local copies, waits for them, and re-layouts: 13.7 us -> none  [the longest x1 6.38 us: shards(): jnp.stack([jnp.take_along_axis(real_flat, direct_index, axis=2), jnp.take...]
    dot_general x22 -> x0, matrix products: 12.5 us -> none  [product(): return jnp.matmul(left_part, right_part, precision=lax.Precision.HIGHEST)]
  transfers between devices with their start and end apart: 8 -> 0, of which waited for: 8 -> 0; matrix products, arithmetic and copies ran while one was open for 0% -> 0% of each run, Pallas kernels for 0% -> 0%
where the time goes in v1:
time: 102 us
  Pallas kernels  98.6 us (97%)
  local copies, waits for them, and re-layouts  3.2 us (3%)
    pallas_call x1, Pallas kernels, shards(): pl.pallas_call(functools.partial(kernel, groups, chains), out_shape=jax.S...  98.6 us
    unnamed x7, local copies, waits for them, and re-layouts  3.2 us

profile of v1, /device:TPU:0, one launch (start us, length us, event | category | flops | bytes accessed | tf_op | source)
XLA Modules:
  0.0 101.8 jit_solution(12015442734091072843)
XLA Ops:
  0.0 0.0 copy-start
  0.0 0.9 copy-done
  0.9 0.0 copy-start.1
  0.9 0.9 copy-done.1
  1.8 0.0 copy-start.2
  1.8 0.8 copy-done.2
  2.6 98.6 %shard_map.37 = f32[2,8,8,128]{3,2,1,0:T(8,128)S(1)} custom-call(f32[2,128,128]{2,1,0:T(8,128)S(1)} %bitcast.5, f32[2,128,128]{2,1,0:T(8,128)S(1)} %bitcast.6, s32[8,1,1024]{2,1,0:T(1,128)S(1)} %bitcast.7), custom_call_target="tpu_custom_call" | custom-call | tf_op jit(solution)/shard_map/pallas_call | solution.py:314
  101.2 0.6 copy.6
Async XLA Ops:
  0.0 0.9 copy-start
  0.9 0.9 copy-start.1
  1.8 0.8 copy-start.2

commit v2 on v1

--- a/solution.py
+++ b/solution.py
@@ -8,7 +8,8 @@
 from jax.sharding import PartitionSpec as P
 
 MESH = pl.DeviceIdType.MESH
-PANEL = 8
+SUB = 8
+PANEL = 32
 BROADENING = 0.04
 
 
@@ -46,83 +47,137 @@
     return jnp.broadcast_to(value[row : row + 1, :], value.shape)
 
 
-def pivot_inverse(real, imag):
+def split(value, terms):
+    pieces = []
+    for _ in range(terms):
+        piece = value.astype(jnp.bfloat16)
+        pieces.append(piece)
+        value = value - piece.astype(jnp.float32)
+    return pieces
+
+
+def narrow_product(left, right):
+    l0, l1, l2 = split(left, 3)
+    r0, r1, r2 = split(right, 3)
+    small = jnp.dot(
+        jnp.concatenate([l0, l2], axis=1),
+        jnp.concatenate([r2, r0], axis=0),
+        preferred_element_type=jnp.float32,
+    )
+    large = jnp.dot(
+        jnp.concatenate([l0, l0, l1, l1], axis=1),
+        jnp.concatenate([r0, r1, r0, r1], axis=0),
+        preferred_element_type=jnp.float32,
+    )
+    return large + small
+
+
+def reciprocal(value):
+    guess = pl.reciprocal(value, approx=True)
+    return guess * (2.0 - value * guess)
+
+
+def pivot_inverse(real, imag, start):
     rows = lax.broadcasted_iota(jnp.int32, real.shape, 0)
-    cols_r = [across(real, c) for c in range(PANEL)]
-    cols_i = [across(imag, c) for c in range(PANEL)]
-    for k in range(PANEL):
+    cols_r = [across(real, start + c) for c in range(SUB)]
+    cols_i = [across(imag, start + c) for c in range(SUB)]
+    for k in range(SUB):
         pivot_r, pivot_i = down(cols_r[k], k), down(cols_i[k], k)
-        scale = 1.0 / (pivot_r * pivot_r + pivot_i * pivot_i)
+        scale = reciprocal(pivot_r * pivot_r + pivot_i * pivot_i)
         inv_r, inv_i = pivot_r * scale, -pivot_i * scale
         here = rows == k
         factor_r = jnp.where(here, -1.0, cols_r[k])
         factor_i = jnp.where(here, 0.0, cols_i[k])
         f_r = factor_r * inv_r - factor_i * inv_i
         f_i = factor_r * inv_i + factor_i * inv_r
-        for c in range(PANEL):
+        for c in range(SUB):
             if c == k:
                 continue
             m_r, m_i = down(cols_r[c], k), down(cols_i[c], k)
             cols_r[c] = jnp.where(here, 0.0, cols_r[c]) - (f_r * m_r - f_i * m_i)
             cols_i[c] = jnp.where(here, 0.0, cols_i[c]) - (f_r * m_i + f_i * m_r)
         cols_r[k], cols_i[k] = -f_r, -f_i
-    return tuple(cols_r) + tuple(cols_i)
+    return cols_r, cols_i
+
+
+def total(terms):
+    while len(terms) > 1:
+        terms = [
+            terms[i] + terms[i + 1] if i + 1 < len(terms) else terms[i]
+            for i in range(0, len(terms), 2)
+        ]
+    return terms[0]
+
+
+def combine(left_r, left_i, right_r, right_i):
+    real = total([a * c - b * d for a, b, c, d in zip(left_r, left_i, right_r, right_i)])
+    imag = total([a * d + b * c for a, b, c, d in zip(left_r, left_i, right_r, right_i)])
+    return real, imag
 
 
 def invert(ref):
     size = ref.shape[-1]
-    count = size // PANEL
-    shape = (PANEL, size)
+    shape = (SUB, size)
     lanes = lax.broadcasted_iota(jnp.int32, shape, 1)
     rows = lax.broadcasted_iota(jnp.int32, shape, 0)
-    low = lanes < PANEL
-    unit = (lanes == rows).astype(jnp.float32)
+    subs = PANEL // SUB
 
     def turn(value):
         return pltpu.roll(value, size - PANEL, 1)
 
-    def step(s, pivot):
-        p_r, p_i = pivot[:PANEL], pivot[PANEL:]
-        here = pl.ds(pl.multiple_of(s * PANEL, PANEL), PANEL)
-        a_r = jnp.where(low, unit, ref[0, here, :])
-        a_i = jnp.where(low, 0.0, ref[1, here, :])
-        r_r, r_i = jnp.zeros(shape, jnp.float32), jnp.zeros(shape, jnp.float32)
-        for c in range(PANEL):
-            b_r, b_i = down(a_r, c), down(a_i, c)
-            r_r = r_r + (p_r[c] * b_r - p_i[c] * b_i)
-            r_i = r_i + (p_r[c] * b_i + p_i[c] * b_r)
-        rb_r = [down(r_r, c) for c in range(PANEL)]
-        rb_i = [down(r_i, c) for c in range(PANEL)]
-
-        def updated(at):
-            x_r, x_i = ref[0, at, :], ref[1, at, :]
-            y_r, y_i = jnp.where(low, 0.0, x_r), jnp.where(low, 0.0, x_i)
-            for c in range(PANEL):
-                c_r, c_i = across(x_r, c), across(x_i, c)
-                y_r = y_r - (c_r * rb_r[c] - c_i * rb_i[c])
-                y_i = y_i - (c_r * rb_i[c] + c_i * rb_r[c])
-            return turn(y_r), turn(y_i)
-
-        following = lax.rem(s + 1, count)
-        ahead = updated(pl.ds(pl.multiple_of(following * PANEL, PANEL), PANEL))
-        later = pivot_inverse(*ahead)
-        for i in range(count):
-            at = pl.ds(i * PANEL, PANEL)
-            z_r, z_i = updated(at)
-            ref[0, at, :] = z_r
-            ref[1, at, :] = z_i
-        ref[0, here, :] = turn(r_r)
-        ref[1, here, :] = turn(r_i)
-        return later
-
-    first = pivot_inverse(ref[0, pl.ds(0, PANEL), :], ref[1, pl.ds(0, PANEL), :])
-    lax.fori_loop(0, count, step, first)
+    def step(p, carry):
+        first = p * PANEL
+        strips = []
+        for j in range(subs):
+            at = pl.ds(pl.multiple_of(first + j * SUB, SUB), SUB)
+            strips.append((ref[0, at, :], ref[1, at, :]))
+        for s in range(subs):
+            start = s * SUB
+            inside = jnp.logical_and(lanes >= start, lanes < start + SUB)
+            x_r, x_i = strips[s]
+            p_r, p_i = pivot_inverse(x_r, x_i, start)
+            a_r = jnp.where(inside, (lanes - start == rows).astype(jnp.float32), x_r)
+            a_i = jnp.where(inside, 0.0, x_i)
+            r_r, r_i = combine(
+                p_r, p_i, [down(a_r, c) for c in range(SUB)], [down(a_i, c) for c in range(SUB)]
+            )
+            b_r = [down(r_r, c) for c in range(SUB)]
+            b_i = [down(r_i, c) for c in range(SUB)]
+            for t in range(1, subs):
+                j = (s + t) % subs
+                x_r, x_i = strips[j]
+                d_r, d_i = combine(
+                    [across(x_r, start + c) for c in range(SUB)],
+                    [across(x_i, start + c) for c in range(SUB)],
+                    b_r,
+                    b_i,
+                )
+                strips[j] = (jnp.where(inside, 0.0, x_r) - d_r, jnp.where(inside, 0.0, x_i) - d_i)
+            strips[s] = (r_r, r_i)
+        p_r = turn(jnp.concatenate([strip[0] for strip in strips], axis=0))
+        p_i = turn(jnp.concatenate([strip[1] for strip in strips], axis=0))
+        m_r, m_i = ref[0], ref[1]
+        change = narrow_product(
+            jnp.concatenate([m_r[:, :PANEL], m_i[:, :PANEL]], axis=1),
+            jnp.concatenate(
+                [jnp.concatenate([p_r, p_i], axis=1), jnp.concatenate([-p_i, p_r], axis=1)], axis=0
+            ),
+        )
+        beyond = lax.broadcasted_iota(jnp.int32, (size, size), 1) >= PANEL
+        ref[0] = turn(jnp.where(beyond, m_r, 0.0)) - change[:, :size]
+        ref[1] = turn(jnp.where(beyond, m_i, 0.0)) - change[:, size:]
+        at = pl.ds(pl.multiple_of(first, PANEL), PANEL)
+        ref[0, at, :] = p_r
+        ref[1, at, :] = p_i
+        return carry
+
+    lax.fori_loop(0, size // PANEL, step, 0)
 
 
 def kernel(
-    groups, chains, onsite, coupling, retained, out,
+    groups, chains, onsite_in, coupling_in, retained_in, out, onsite, coupling, retained,
     base, work, toward, left, prev, sigma_in, green_in, sigma_out, picked, table, received,
-    u_send, u_recv, s_send, s_recv, g_send, g_recv, a_send, a_recv,
+    u_send, u_recv, s_send, s_recv, g_send, g_recv, a_send, a_recv, fetch,
 ):
     size = onsite.shape[-1]
     me = lax.axis_index("energy")
@@ -135,6 +190,13 @@
     middle = depth == half - 1
     at_edge = depth == 0
 
+    get_onsite = pltpu.make_async_copy(onsite_in, onsite, fetch.at[0])
+    get_coupling = pltpu.make_async_copy(coupling_in, coupling, fetch.at[1])
+    get_retained = pltpu.make_async_copy(retained_in, retained, fetch.at[2])
+    get_onsite.start()
+    get_coupling.start()
+    get_retained.start()
+
     barrier = pltpu.get_barrier_semaphore()
 
     def greet(energy, chain):
@@ -162,6 +224,7 @@
     def sigma_arrival(which):
         copy(sigma_out, sigma_in.at[which], s_send, s_recv.at[which], me, inner).wait_recv()
 
+    get_onsite.wait()
     diagonal = (
         lax.broadcasted_iota(jnp.int32, (size, size), 0)
         == lax.broadcasted_iota(jnp.int32, (size, size), 1)
@@ -170,6 +233,8 @@
     base[0] = energy * diagonal - 0.5 * (onsite[0] + onsite[0].T)
     base[1] = BROADENING * diagonal - 0.5 * (onsite[1] - onsite[1].T)
 
+    get_coupling.wait()
+
     @pl.when(pos == chains - 1)
     def _():
         coupler = load(coupling)
@@ -223,6 +288,8 @@
     @pl.when(jnp.logical_not(at_edge))
     def _():
         green_copy.start()
+
+    get_retained.wait()
 
     full = load(work)
     planes = jnp.concatenate([full[0], full[1], full[0].T, full[1].T], axis=0)
@@ -314,16 +381,17 @@
     result = pl.pallas_call(
         functools.partial(kernel, groups, chains),
         out_shape=jax.ShapeDtypeStruct((2, groups, columns // 128, 128), jnp.float32),
-        in_specs=[pl.BlockSpec(memory_space=pltpu.VMEM)] * 3,
+        in_specs=[pl.BlockSpec(memory_space=pl.ANY)] * 3,
         out_specs=pl.BlockSpec(memory_space=pltpu.VMEM),
         scratch_shapes=[
+            block, block, pltpu.VMEM((groups, 1, columns), jnp.int32),
             block, block, block, block, block,
             pltpu.VMEM((2, 2, size, size), jnp.float32), block, block,
             picks,
             pltpu.VMEM((4 * size, 2 * size), jnp.bfloat16),
             picks,
             dma(()), dma(()), dma(()), dma((2,)), dma(()), dma(()),
-            dma((groups,)), dma((groups,)),
+            dma((groups,)), dma((groups,)), dma((3,)),
         ],
         compiler_params=pltpu.CompilerParams(
             collective_id=0, has_side_effects=True, vmem_limit_bytes=32 * 1024 * 1024

time: 102 us -> 50.9 us (0.50)
  Pallas kernels: 98.6 us -> 47.5 us
    pallas_call x1, Pallas kernels: 98.6 us -> 47.5 us  [shards(): pl.pallas_call(functools.partial(kernel, groups, chains), out_shape=jax.S...]
where the time goes in v2:
time: 50.9 us; the launch traced here: 50.7 us
  Pallas kernels  47.5 us (93%)
  local copies, waits for them, and re-layouts  3.2 us (6%)
    pallas_call x1, Pallas kernels, shards(): pl.pallas_call(functools.partial(kernel, groups, chains), out_shape=jax.S...  47.5 us
    unnamed x7, local copies, waits for them, and re-layouts  3.2 us

profile of v2, /device:TPU:0, one launch (start us, length us, event | category | flops | bytes accessed | tf_op | source)
XLA Modules:
  0.0 50.7 jit_solution(15663819647853429377)
XLA Ops:
  0.0 0.0 copy-start
  0.0 0.9 %copy-done = f32[1,2,128,128]{3,2,1,0:T(8,128)S(1)} copy-done((f32[1,2,128,128]{3,2,1,0:T(8,128)S(1)}, f32[1,2,128,128]{3,2,1,0:T(8,128)}, u32[]{:S(2)}) %copy-start) | copy-done | bytes 131096
  0.9 0.0 copy-start.1
  0.9 0.9 %copy-done.1 = f32[1,2,128,128]{3,2,1,0:T(8,128)S(1)} copy-done((f32[1,2,128,128]{3,2,1,0:T(8,128)S(1)}, f32[1,2,128,128]{3,2,1,0:T(8,128)}, u32[]{:S(2)}) %copy-start.1) | copy-done | bytes 131096
  1.8 0.0 copy-start.2
  1.8 0.8 %copy-done.2 = s32[1,8192]{1,0:T(1,128)S(1)} copy-done((s32[1,8192]{1,0:T(1,128)S(1)}, s32[1,8192]{1,0:T(1,128)}, u32[]{:S(2)}) %copy-start.2) | copy-done | bytes 32792
  2.6 47.5 %shard_map.37 = f32[2,8,8,128]{3,2,1,0:T(8,128)S(1)} custom-call(f32[2,128,128]{2,1,0:T(8,128)S(1)} %bitcast.5, f32[2,128,128]{2,1,0:T(8,128)S(1)} %bitcast.6, s32[8,1,1024]{2,1,0:T(1,128)S(1)} %bitcast.7), custom_call_target="tpu_custom_call" | custom-call | tf_op jit(solution)/shard_map/pallas_call | solution.py:381
  50.1 0.6 %copy.6 = f32[2,8,1,1024]{3,2,1,0:T(1,128)} copy(f32[2,8,1,1024]{3,2,1,0:T(1,128)S(1)} %bitcast.4) | data formatting | bytes 131072
Async XLA Ops:
  0.0 0.9 %copy-start = (f32[1,2,128,128]{3,2,1,0:T(8,128)S(1)}, f32[1,2,128,128]{3,2,1,0:T(8,128)}, u32[]{:S(2)}) copy-start(f32[1,2,128,128]{3,2,1,0:T(8,128)} %param.3) | copy-start | bytes 393220
  0.9 0.9 %copy-start.1 = (f32[1,2,128,128]{3,2,1,0:T(8,128)S(1)}, f32[1,2,128,128]{3,2,1,0:T(8,128)}, u32[]{:S(2)}) copy-start(f32[1,2,128,128]{3,2,1,0:T(8,128)} %param.4) | copy-start | bytes 393220
  1.8 0.8 %copy-start.2 = (s32[1,8192]{1,0:T(1,128)S(1)}, s32[1,8192]{1,0:T(1,128)}, u32[]{:S(2)}) copy-start(s32[1,8192]{1,0:T(1,128)} %param.5) | copy-start | bytes 98308

commit v3 on v2

--- a/solution.py
+++ b/solution.py
@@ -13,15 +13,21 @@
 BROADENING = 0.04
 
 
-def product(left, right):
+def product(left, right, exact=True):
     wide = jnp.concatenate(left, axis=1)
     real, imag = right
     tall = jnp.concatenate(
         [jnp.concatenate([real, imag], axis=1), jnp.concatenate([-imag, real], axis=1)], axis=0
     )
-    both = jnp.dot(
-        wide, tall, precision=lax.Precision.HIGHEST, preferred_element_type=jnp.float32
-    )
+    if exact:
+        both = jnp.dot(
+            wide, tall, precision=lax.Precision.HIGHEST, preferred_element_type=jnp.float32
+        )
+    else:
+        w0, w1 = split(wide, 2)
+        t0, t1 = split(tall, 2)
+        dot = functools.partial(jnp.dot, preferred_element_type=jnp.float32)
+        both = dot(w0, t0) + (dot(w0, t1) + dot(w1, t0))
     size = real.shape[1]
     return both[:, :size], both[:, size:]
 
@@ -81,22 +87,37 @@
     rows = lax.broadcasted_iota(jnp.int32, real.shape, 0)
     cols_r = [across(real, start + c) for c in range(SUB)]
     cols_i = [across(imag, start + c) for c in range(SUB)]
-    for k in range(SUB):
-        pivot_r, pivot_i = down(cols_r[k], k), down(cols_i[k], k)
-        scale = reciprocal(pivot_r * pivot_r + pivot_i * pivot_i)
-        inv_r, inv_i = pivot_r * scale, -pivot_i * scale
-        here = rows == k
-        factor_r = jnp.where(here, -1.0, cols_r[k])
-        factor_i = jnp.where(here, 0.0, cols_i[k])
-        f_r = factor_r * inv_r - factor_i * inv_i
-        f_i = factor_r * inv_i + factor_i * inv_r
+    for k in range(0, SUB, 2):
+        a_r, a_i = down(cols_r[k], k), down(cols_i[k], k)
+        b_r, b_i = down(cols_r[k + 1], k), down(cols_i[k + 1], k)
+        c_r, c_i = down(cols_r[k], k + 1), down(cols_i[k], k + 1)
+        d_r, d_i = down(cols_r[k + 1], k + 1), down(cols_i[k + 1], k + 1)
+        det_r = (a_r * d_r - a_i * d_i) - (b_r * c_r - b_i * c_i)
+        det_i = (a_r * d_i + a_i * d_r) - (b_r * c_i + b_i * c_r)
+        scale = reciprocal(det_r * det_r + det_i * det_i)
+        one, two = rows == k, rows == k + 1
+        either = jnp.logical_or(one, two)
+        e_r = jnp.where(one, -1.0, jnp.where(two, 0.0, cols_r[k]))
+        e_i = jnp.where(either, 0.0, cols_i[k])
+        f_r = jnp.where(two, -1.0, jnp.where(one, 0.0, cols_r[k + 1]))
+        f_i = jnp.where(either, 0.0, cols_i[k + 1])
+        u_r = (e_r * d_r - e_i * d_i) - (f_r * c_r - f_i * c_i)
+        u_i = (e_r * d_i + e_i * d_r) - (f_r * c_i + f_i * c_r)
+        v_r = (f_r * a_r - f_i * a_i) - (e_r * b_r - e_i * b_i)
+        v_i = (f_r * a_i + f_i * a_r) - (e_r * b_i + e_i * b_r)
+        u_r, u_i = u_r * det_r + u_i * det_i, u_i * det_r - u_r * det_i
+        v_r, v_i = v_r * det_r + v_i * det_i, v_i * det_r - v_r * det_i
         for c in range(SUB):
-            if c == k:
+            if c in (k, k + 1):
                 continue
             m_r, m_i = down(cols_r[c], k), down(cols_i[c], k)
-            cols_r[c] = jnp.where(here, 0.0, cols_r[c]) - (f_r * m_r - f_i * m_i)
-            cols_i[c] = jnp.where(here, 0.0, cols_i[c]) - (f_r * m_i + f_i * m_r)
-        cols_r[k], cols_i[k] = -f_r, -f_i
+            n_r, n_i = down(cols_r[c], k + 1), down(cols_i[c], k + 1)
+            w_r = (u_r * m_r - u_i * m_i) + (v_r * n_r - v_i * n_i)
+            w_i = (u_r * m_i + u_i * m_r) + (v_r * n_i + v_i * n_r)
+            cols_r[c] = jnp.where(either, 0.0, cols_r[c]) - scale * w_r
+            cols_i[c] = jnp.where(either, 0.0, cols_i[c]) - scale * w_i
+        cols_r[k], cols_i[k] = -scale * u_r, -scale * u_i
+        cols_r[k + 1], cols_i[k + 1] = -scale * v_r, -scale * v_i
     return cols_r, cols_i
 
 
@@ -177,7 +198,7 @@
 def kernel(
     groups, chains, onsite_in, coupling_in, retained_in, out, onsite, coupling, retained,
     base, work, toward, left, prev, sigma_in, green_in, sigma_out, picked, table, received,
-    u_send, u_recv, s_send, s_recv, g_send, g_recv, a_send, a_recv, fetch,
+    u_send, u_recv, s_send, s_recv, g_send, g_recv, a_send, a_recv, fetch, hot,
 ):
     size = onsite.shape[-1]
     me = lax.axis_index("energy")
@@ -242,7 +263,10 @@
         base[0] = base[0] - 0.5 * square[1]
         base[1] = base[1] + 0.5 * square[0]
 
-    pl.semaphore_wait(barrier, groups + jnp.where(at_edge, 0, 1))
+    @pl.when(jnp.logical_not(at_edge))
+    def _():
+        pl.semaphore_wait(barrier, groups + 1)
+
 
     sends_coupling = jnp.logical_and(pos >= half - 1, pos < chains - 1)
 
@@ -250,8 +274,24 @@
     def _():
         coupling_copy.start()
 
+    columns = retained.shape[-1]
+    across_rows = columns // 128
+
+    def prepare():
+        get_retained.wait()
+        spot = lax.broadcasted_iota(jnp.int32, (size, columns), 0)
+
+        def fill(group, carry):
+            one = (spot == retained[group] % size).astype(jnp.float32).astype(jnp.bfloat16)
+            hot[group, pl.ds(0, size), :] = one
+            hot[group, pl.ds(size, size), :] = one
+            return carry
+
+        lax.fori_loop(0, groups, fill, 0)
+
     @pl.when(jnp.logical_not(at_edge))
     def _():
+        prepare()
         sigma_arrival(0)
         base[...] = base[...] - sigma_in[0]
 
@@ -269,7 +309,16 @@
 
     store(left, product(load(work), load(toward)))
     store(sigma_out, product(adjoint(load(toward)), load(left)))
+
+    @pl.when(at_edge)
+    def _():
+        pl.semaphore_wait(barrier, groups)
+
     sigma_copy.start()
+
+    @pl.when(at_edge)
+    def _():
+        prepare()
 
     @pl.when(middle)
     def _():
@@ -281,32 +330,25 @@
     def _():
         right = product(adjoint(load(toward)), load(work))
         green_copy.wait_recv()
-        change = product(product(load(left), load(green_in)), right)
+        change = product(product(load(left), load(green_in), False), right, False)
         work[0] = work[0] + change[0]
         work[1] = work[1] + change[1]
 
     @pl.when(jnp.logical_not(at_edge))
     def _():
         green_copy.start()
-
-    get_retained.wait()
 
     full = load(work)
     planes = jnp.concatenate([full[0], full[1], full[0].T, full[1].T], axis=0)
     high = planes.astype(jnp.bfloat16)
     low = (planes - high.astype(jnp.float32)).astype(jnp.bfloat16)
     table[...] = jnp.concatenate([high, low], axis=1)
-    columns = retained.shape[-1]
-    across_rows = columns // 128
 
     def pick(group, target, place):
         chosen = retained[group]
         spot = lax.broadcasted_iota(jnp.int32, (size, columns), 0)
-        hot = (spot == chosen % size).astype(jnp.float32).astype(jnp.bfloat16)
         keep = spot == chosen // size
-        rows = jnp.dot(
-            table[...], jnp.concatenate([hot, hot], axis=0), preferred_element_type=jnp.float32
-        )
+        rows = jnp.dot(table[...], hot[group], preferred_element_type=jnp.float32)
         for p in range(4):
             part = jnp.where(keep, rows[p * size : (p + 1) * size], 0.0)
             line = jnp.sum(part, axis=0, keepdims=True)
@@ -381,7 +423,7 @@
     result = pl.pallas_call(
         functools.partial(kernel, groups, chains),
         out_shape=jax.ShapeDtypeStruct((2, groups, columns // 128, 128), jnp.float32),
-        in_specs=[pl.BlockSpec(memory_space=pl.ANY)] * 3,
+        in_specs=[pl.BlockSpec(memory_space=pltpu.HBM)] * 3,
         out_specs=pl.BlockSpec(memory_space=pltpu.VMEM),
         scratch_shapes=[
             block, block, pltpu.VMEM((groups, 1, columns), jnp.int32),
@@ -392,10 +434,9 @@
             picks,
             dma(()), dma(()), dma(()), dma((2,)), dma(()), dma(()),
             dma((groups,)), dma((groups,)), dma((3,)),
+            pltpu.VMEM((groups, 2 * size, columns), jnp.bfloat16),
         ],
-        compiler_params=pltpu.CompilerParams(
-            collective_id=0, has_side_effects=True, vmem_limit_bytes=32 * 1024 * 1024
-        ),
+        compiler_params=pltpu.CompilerParams(collective_id=0, has_side_effects=True),
     )(onsite[0], coupling[0], retained.reshape(groups, 1, columns))
     return result.reshape(2, groups, 1, columns)
 

time: 50.9 us -> 46.7 us (0.917)
  Pallas kernels: 47.5 us -> 45 us
  local copies, waits for them, and re-layouts: 3.2 us -> 1.47 us
    pallas_call x1, Pallas kernels: 47.5 us -> 45 us  [shards(): pl.pallas_call(functools.partial(kernel, groups, chains), out_shape=jax.S...]
    unnamed x7 -> x1, local copies, waits for them, and re-layouts: 3.2 us -> 1.47 us
where the time goes in v3:
time: 46.7 us; the launch traced here: 46.5 us
  Pallas kernels  45 us (96%)
  local copies, waits for them, and re-layouts  1.47 us (3%)
    pallas_call x1, Pallas kernels, shards(): pl.pallas_call(functools.partial(kernel, groups, chains), out_shape=jax.S...  45 us
    unnamed x1, local copies, waits for them, and re-layouts  1.47 us

profile of v3, /device:TPU:0, one launch (start us, length us, event | category | flops | bytes accessed | tf_op | source)
XLA Modules:
  0.0 46.5 jit_solution(16738338606622468477)
XLA Ops:
  0.0 45.0 %shard_map.37 = f32[2,8,8,128]{3,2,1,0:T(8,128)} custom-call(f32[2,128,128]{2,1,0:T(8,128)} %bitcast.5, f32[2,128,128]{2,1,0:T(8,128)} %bitcast.6, s32[8,1,1024]{2,1,0:T(1,128)} %bitcast.7), custom_call_target="tpu_custom_call" | custom-call | tf_op jit(solution)/shard_map/pallas_call | solution.py:423
  45.0 1.5 %copy.6 = f32[2,8,1,1024]{3,2,1,0:T(1,128)} copy(f32[2,8,1,1024]{3,2,1,0:T(1,128)} %bitcast.4) | data formatting | bytes 131072

commit v4 on v3

--- a/solution.py
+++ b/solution.py
@@ -10,6 +10,8 @@
 MESH = pl.DeviceIdType.MESH
 SUB = 8
 PANEL = 32
+CHUNKS = 4
+GRANT = 64 * 1024 * 1024 - 80 * 1024
 BROADENING = 0.04
 
 
@@ -152,11 +154,16 @@
         for j in range(subs):
             at = pl.ds(pl.multiple_of(first + j * SUB, SUB), SUB)
             strips.append((ref[0, at, :], ref[1, at, :]))
+        opening = strips[0]
+        strips = [(turn(strip[0]), turn(strip[1])) for strip in strips]
         for s in range(subs):
-            start = s * SUB
+            start = size - PANEL + s * SUB
             inside = jnp.logical_and(lanes >= start, lanes < start + SUB)
             x_r, x_i = strips[s]
-            p_r, p_i = pivot_inverse(x_r, x_i, start)
+            if s == 0:
+                p_r, p_i = pivot_inverse(opening[0], opening[1], 0)
+            else:
+                p_r, p_i = pivot_inverse(x_r, x_i, start)
             a_r = jnp.where(inside, (lanes - start == rows).astype(jnp.float32), x_r)
             a_i = jnp.where(inside, 0.0, x_i)
             r_r, r_i = combine(
@@ -175,8 +182,8 @@
                 )
                 strips[j] = (jnp.where(inside, 0.0, x_r) - d_r, jnp.where(inside, 0.0, x_i) - d_i)
             strips[s] = (r_r, r_i)
-        p_r = turn(jnp.concatenate([strip[0] for strip in strips], axis=0))
-        p_i = turn(jnp.concatenate([strip[1] for strip in strips], axis=0))
+        p_r = jnp.concatenate([strip[0] for strip in strips], axis=0)
+        p_i = jnp.concatenate([strip[1] for strip in strips], axis=0)
         m_r, m_i = ref[0], ref[1]
         change = narrow_product(
             jnp.concatenate([m_r[:, :PANEL], m_i[:, :PANEL]], axis=1),
@@ -199,6 +206,7 @@
     groups, chains, onsite_in, coupling_in, retained_in, out, onsite, coupling, retained,
     base, work, toward, left, prev, sigma_in, green_in, sigma_out, picked, table, received,
     u_send, u_recv, s_send, s_recv, g_send, g_recv, a_send, a_recv, fetch, hot,
+    core, ship, right, c_send, c_recv,
 ):
     size = onsite.shape[-1]
     me = lax.axis_index("energy")
@@ -239,11 +247,25 @@
 
     coupling_copy = copy(coupling, prev, u_send, u_recv, me, lax.rem(pos + 1, chains))
     slot = jnp.where(middle, 1, 0)
-    sigma_copy = copy(sigma_out, sigma_in.at[slot], s_send, s_recv.at[slot], me, inner)
-    green_copy = copy(work, green_in, g_send, g_recv, me, jnp.clip(outer, 0, chains - 1))
-
-    def sigma_arrival(which):
-        copy(sigma_out, sigma_in.at[which], s_send, s_recv.at[which], me, inner).wait_recv()
+    strip = size // CHUNKS
+    beyond = jnp.clip(outer, 0, chains - 1)
+
+    def part(ref, c):
+        return ref.at[:, pl.ds(c * strip, strip), :]
+
+    def sigma_copy(which, c):
+        return copy(
+            part(sigma_out, c), part(sigma_in.at[which], c), s_send.at[c], s_recv.at[which, c],
+            me, inner,
+        )
+
+    def core_copy(c):
+        return copy(part(ship, c), part(core, c), c_send.at[c], c_recv.at[c], me, beyond)
+
+    if half > 2:
+        green_copy = copy(work, green_in, g_send, g_recv, me, beyond)
+    near = depth == half - 2
+    passes_on = jnp.logical_and(jnp.logical_not(at_edge), jnp.logical_not(middle))
 
     get_onsite.wait()
     diagonal = (
@@ -292,7 +314,8 @@
     @pl.when(jnp.logical_not(at_edge))
     def _():
         prepare()
-        sigma_arrival(0)
+        for c in range(CHUNKS):
+            sigma_copy(0, c).wait_recv()
         base[...] = base[...] - sigma_in[0]
 
     work[...] = base[...]
@@ -314,7 +337,8 @@
     def _():
         pl.semaphore_wait(barrier, groups)
 
-    sigma_copy.start()
+    for c in range(CHUNKS):
+        sigma_copy(slot, c).start()
 
     @pl.when(at_edge)
     def _():
@@ -322,21 +346,49 @@
 
     @pl.when(middle)
     def _():
-        sigma_arrival(1)
-        work[...] = base[...] - sigma_in[1]
-        invert(work)
+        for c in range(CHUNKS):
+            sigma_copy(1, c).wait_recv()
+            at = pl.ds(c * strip, strip)
+            last = base[:, at, :] - sigma_in[1, :, at, :]
+            ship[:, at, :] = last
+            core_copy(c).start()
+            core[:, at, :] = last
 
     @pl.when(jnp.logical_not(middle))
     def _():
-        right = product(adjoint(load(toward)), load(work))
-        green_copy.wait_recv()
-        change = product(product(load(left), load(green_in), False), right, False)
+        store(right, product(adjoint(load(toward)), load(work)))
+
+    def add_change(following):
+        change = product(product(load(left), load(following), False), load(right), False)
         work[0] = work[0] + change[0]
         work[1] = work[1] + change[1]
 
-    @pl.when(jnp.logical_not(at_edge))
-    def _():
-        green_copy.start()
+    @pl.when(near)
+    def _():
+        for c in range(CHUNKS):
+            core_copy(c).wait_recv()
+
+    @pl.when(jnp.logical_or(middle, near))
+    def _():
+        invert(core)
+
+    @pl.when(middle)
+    def _():
+        work[...] = core[...]
+
+    @pl.when(near)
+    def _():
+        add_change(core)
+
+    if half > 2:
+        @pl.when(depth < half - 2)
+        def _():
+            green_copy.wait_recv()
+            add_change(green_in)
+
+        @pl.when(passes_on)
+        def _():
+            green_copy.start()
 
     full = load(work)
     planes = jnp.concatenate([full[0], full[1], full[0].T, full[1].T], axis=0)
@@ -395,15 +447,22 @@
 
     lax.fori_loop(0, groups, shift_step, 0)
 
-    sigma_copy.wait_send()
+    for c in range(CHUNKS):
+        sigma_copy(slot, c).wait_send()
+
+    @pl.when(middle)
+    def _():
+        for c in range(CHUNKS):
+            core_copy(c).wait_send()
 
     @pl.when(sends_coupling)
     def _():
         coupling_copy.wait_send()
 
-    @pl.when(jnp.logical_not(at_edge))
-    def _():
-        green_copy.wait_send()
+    if half > 2:
+        @pl.when(passes_on)
+        def _():
+            green_copy.wait_send()
 
     def leave_step(t, carry):
         exchange(t).wait_send()
@@ -432,11 +491,14 @@
             picks,
             pltpu.VMEM((4 * size, 2 * size), jnp.bfloat16),
             picks,
-            dma(()), dma(()), dma(()), dma((2,)), dma(()), dma(()),
+            dma(()), dma(()), dma((CHUNKS,)), dma((2, CHUNKS)), dma(()), dma(()),
             dma((groups,)), dma((groups,)), dma((3,)),
             pltpu.VMEM((groups, 2 * size, columns), jnp.bfloat16),
+            block, block, block, dma((CHUNKS,)), dma((CHUNKS,)),
         ],
-        compiler_params=pltpu.CompilerParams(collective_id=0, has_side_effects=True),
+        compiler_params=pltpu.CompilerParams(
+            collective_id=0, has_side_effects=True, vmem_limit_bytes=GRANT
+        ),
     )(onsite[0], coupling[0], retained.reshape(groups, 1, columns))
     return result.reshape(2, groups, 1, columns)
 

time: 46.7 us -> 44.5 us (0.953)
  Pallas kernels: 45 us -> 42.8 us
    pallas_call x1, Pallas kernels: 45 us -> 42.8 us  [shards(): pl.pallas_call(functools.partial(kernel, groups, chains), out_shape=jax.S...]
where the time goes in v4:
time: 44.5 us; the launch traced here: 44.3 us
  Pallas kernels  42.8 us (96%)
  local copies, waits for them, and re-layouts  1.47 us (3%)
    pallas_call x1, Pallas kernels, shards(): pl.pallas_call(functools.partial(kernel, groups, chains), out_shape=jax.S...  42.8 us
    unnamed x1, local copies, waits for them, and re-layouts  1.47 us

profile of v4, /device:TPU:0, one launch (start us, length us, event | category | flops | bytes accessed | tf_op | source)
XLA Modules:
  0.0 44.3 jit_solution(11533058027347872435)
XLA Ops:
  0.0 42.8 %shard_map.37 = f32[2,8,8,128]{3,2,1,0:T(8,128)} custom-call(f32[2,128,128]{2,1,0:T(8,128)} %bitcast.5, f32[2,128,128]{2,1,0:T(8,128)} %bitcast.6, s32[8,1,1024]{2,1,0:T(1,128)} %bitcast.7), custom_call_target="tpu_custom_call" | custom-call | tf_op jit(solution)/shard_map/pallas_call | solution.py:482
  42.8 1.5 %copy.6 = f32[2,8,1,1024]{3,2,1,0:T(1,128)} copy(f32[2,8,1,1024]{3,2,1,0:T(1,128)} %bitcast.4) | data formatting | bytes 131072

commit v5 on v4

--- a/solution.py
+++ b/solution.py
@@ -9,9 +9,9 @@
 
 MESH = pl.DeviceIdType.MESH
 SUB = 8
-PANEL = 32
+PANEL = 64
 CHUNKS = 4
-GRANT = 64 * 1024 * 1024 - 80 * 1024
+GRANT = 64 * 1024 * 1024 - 256 * 1024
 BROADENING = 0.04
 
 
@@ -481,7 +481,7 @@
     dma = pltpu.SemaphoreType.DMA
     result = pl.pallas_call(
         functools.partial(kernel, groups, chains),
-        out_shape=jax.ShapeDtypeStruct((2, groups, columns // 128, 128), jnp.float32),
+        out_shape=pltpu.VMEM((2, groups, columns // 128, 128), jnp.float32),
         in_specs=[pl.BlockSpec(memory_space=pltpu.HBM)] * 3,
         out_specs=pl.BlockSpec(memory_space=pltpu.VMEM),
         scratch_shapes=[

time: 44.5 us -> 42.2 us (0.948)
  Pallas kernels: 42.8 us -> 41.4 us
  local copies, waits for them, and re-layouts: 1.47 us -> 0.63 us
    pallas_call x1, Pallas kernels: 42.8 us -> 41.4 us  [shards(): pl.pallas_call(functools.partial(kernel, groups, chains), out_shape=pltpu...]
    unnamed x1, local copies, waits for them, and re-layouts: 1.47 us -> 0.63 us
where the time goes in v5:
time: 42.2 us; the launch traced here: 42 us
  Pallas kernels  41.4 us (98%)
  local copies, waits for them, and re-layouts  0.63 us (1%)
    pallas_call x1, Pallas kernels, shards(): pl.pallas_call(functools.partial(kernel, groups, chains), out_shape=pltpu...  41.4 us

profile of v5, /device:TPU:0, one launch (start us, length us, event | category | flops | bytes accessed | tf_op | source)
XLA Modules:
  0.0 42.0 jit_solution(8583178008951396236)
XLA Ops:
  0.0 41.4 %shard_map.37 = f32[2,8,8,128]{3,2,1,0:T(8,128)S(1)} custom-call(f32[2,128,128]{2,1,0:T(8,128)} %bitcast.5, f32[2,128,128]{2,1,0:T(8,128)} %bitcast.6, s32[8,1,1024]{2,1,0:T(1,128)} %bitcast.7), custom_call_target="tpu_custom_call" | custom-call | tf_op jit(solution)/shard_map/pallas_call | solution.py:482
  41.4 0.6 %copy.6 = f32[2,8,1,1024]{3,2,1,0:T(1,128)} copy(f32[2,8,1,1024]{3,2,1,0:T(1,128)S(1)} %bitcast.4) | data formatting | bytes 131072

commit v6 on v5

--- a/solution.py
+++ b/solution.py
@@ -206,7 +206,7 @@
     groups, chains, onsite_in, coupling_in, retained_in, out, onsite, coupling, retained,
     base, work, toward, left, prev, sigma_in, green_in, sigma_out, picked, table, received,
     u_send, u_recv, s_send, s_recv, g_send, g_recv, a_send, a_recv, fetch, hot,
-    core, ship, right, c_send, c_recv,
+    core, ship, right, c_send, c_recv, landing,
 ):
     size = onsite.shape[-1]
     me = lax.axis_index("energy")
@@ -260,7 +260,7 @@
         )
 
     def core_copy(c):
-        return copy(part(ship, c), part(core, c), c_send.at[c], c_recv.at[c], me, beyond)
+        return copy(part(ship, c), part(landing, c), c_send.at[c], c_recv.at[c], me, beyond)
 
     if half > 2:
         green_copy = copy(work, green_in, g_send, g_recv, me, beyond)
@@ -318,59 +318,74 @@
             sigma_copy(0, c).wait_recv()
         base[...] = base[...] - sigma_in[0]
 
-    work[...] = base[...]
-    invert(work)
-
-    @pl.when(in_left)
-    def _():
-        toward[...] = coupling[...]
-
-    @pl.when(jnp.logical_not(in_left))
-    def _():
-        coupling_copy.wait_recv()
-        store(toward, adjoint(load(prev)))
-
-    store(left, product(load(work), load(toward)))
-    store(sigma_out, product(adjoint(load(toward)), load(left)))
-
-    @pl.when(at_edge)
-    def _():
-        pl.semaphore_wait(barrier, groups)
-
-    for c in range(CHUNKS):
-        sigma_copy(slot, c).start()
-
-    @pl.when(at_edge)
-    def _():
-        prepare()
-
-    @pl.when(middle)
-    def _():
-        for c in range(CHUNKS):
-            sigma_copy(1, c).wait_recv()
-            at = pl.ds(c * strip, strip)
-            last = base[:, at, :] - sigma_in[1, :, at, :]
-            ship[:, at, :] = last
-            core_copy(c).start()
-            core[:, at, :] = last
-
-    @pl.when(jnp.logical_not(middle))
-    def _():
-        store(right, product(adjoint(load(toward)), load(work)))
-
     def add_change(following):
         change = product(product(load(left), load(following), False), load(right), False)
         work[0] = work[0] + change[0]
         work[1] = work[1] + change[1]
 
-    @pl.when(near)
-    def _():
+    def first_round():
+        work[...] = core[...]
+
+        @pl.when(in_left)
+        def _():
+            toward[...] = coupling[...]
+
+        @pl.when(jnp.logical_not(in_left))
+        def _():
+            coupling_copy.wait_recv()
+            store(toward, adjoint(load(prev)))
+
+        store(left, product(load(work), load(toward)))
+        store(sigma_out, product(adjoint(load(toward)), load(left)))
+
+        @pl.when(at_edge)
+        def _():
+            pl.semaphore_wait(barrier, groups)
+
         for c in range(CHUNKS):
-            core_copy(c).wait_recv()
-
-    @pl.when(jnp.logical_or(middle, near))
-    def _():
-        invert(core)
+            sigma_copy(slot, c).start()
+
+        @pl.when(at_edge)
+        def _():
+            prepare()
+
+        @pl.when(middle)
+        def _():
+            for c in range(CHUNKS):
+                sigma_copy(1, c).wait_recv()
+                at = pl.ds(c * strip, strip)
+                last = base[:, at, :] - sigma_in[1, :, at, :]
+                ship[:, at, :] = last
+                core_copy(c).start()
+                core[:, at, :] = last
+
+        @pl.when(jnp.logical_not(middle))
+        def _():
+            store(right, product(adjoint(load(toward)), load(work)))
+
+        @pl.when(near)
+        def _():
+            for c in range(CHUNKS):
+                core_copy(c).wait_recv()
+            core[...] = landing[...]
+
+
+    core[...] = base[...]
+
+    def round_step(index, carry):
+        first = index == 0
+
+        @pl.when(jnp.logical_or(first, jnp.logical_or(middle, near)))
+        def _():
+            invert(core)
+
+        @pl.when(first)
+        def _():
+            first_round()
+
+        return carry
+
+    lax.fori_loop(0, 2, round_step, 0)
 
     @pl.when(middle)
     def _():
@@ -413,14 +428,20 @@
             picked.at[peer], received.at[me], a_send.at[peer], a_recv.at[me], peer, pos
         )
 
-    def send_step(t, carry):
-        peer = lax.rem(me + t, groups)
-        pick(peer, picked, peer)
-        exchange(t).start()
+    def send_step(step, carry):
+        peers = [lax.rem(me + 2 * step + 1 + t, groups) for t in range(2)]
+        for peer in peers:
+            pick(peer, picked, peer)
+        exchange(2 * step + 1).start()
+
+        @pl.when(step < groups // 2 - 1)
+        def _():
+            exchange(2 * step + 2).start()
+
         return carry
 
-    lax.fori_loop(1, groups, send_step, 0)
-    pick(me, received, me)
+    lax.fori_loop(0, groups // 2, send_step, 0)
+    received[me] = picked[me]
 
     def arrive_step(t, carry):
         source = lax.rem(me + t, groups)
@@ -494,7 +515,7 @@
             dma(()), dma(()), dma((CHUNKS,)), dma((2, CHUNKS)), dma(()), dma(()),
             dma((groups,)), dma((groups,)), dma((3,)),
             pltpu.VMEM((groups, 2 * size, columns), jnp.bfloat16),
-            block, block, block, dma((CHUNKS,)), dma((CHUNKS,)),
+            block, block, block, dma((CHUNKS,)), dma((CHUNKS,)), block,
         ],
         compiler_params=pltpu.CompilerParams(
             collective_id=0, has_side_effects=True, vmem_limit_bytes=GRANT

time: 42.2 us -> 42 us (level)
  no operation moved by 1% of the time
where the time goes in v6:
time: 42 us; the launch traced here: 41.7 us
  Pallas kernels  41.1 us (98%)
  local copies, waits for them, and re-layouts  0.63 us (2%)
    pallas_call x1, Pallas kernels, shards(): pl.pallas_call(functools.partial(kernel, groups, chains), out_shape=pltpu...  41.1 us

profile of v6, /device:TPU:0, one launch (start us, length us, event | category | flops | bytes accessed | tf_op | source)
XLA Modules:
  0.0 41.7 jit_solution(18103859520977578050)
XLA Ops:
  0.0 41.1 %shard_map.37 = f32[2,8,8,128]{3,2,1,0:T(8,128)S(1)} custom-call(f32[2,128,128]{2,1,0:T(8,128)} %bitcast.5, f32[2,128,128]{2,1,0:T(8,128)} %bitcast.6, s32[8,1,1024]{2,1,0:T(1,128)} %bitcast.7), custom_call_target="tpu_custom_call" | custom-call | tf_op jit(solution)/shard_map/pallas_call | solution.py:503
  41.1 0.6 %copy.6 = f32[2,8,1,1024]{3,2,1,0:T(1,128)} copy(f32[2,8,1,1024]{3,2,1,0:T(1,128)S(1)} %bitcast.4) | data formatting | bytes 131072

commit v7 on v6

--- a/solution.py
+++ b/solution.py
@@ -15,7 +15,7 @@
 BROADENING = 0.04
 
 
-def product(left, right, exact=True):
+def product(left, right, exact=False):
     wide = jnp.concatenate(left, axis=1)
     real, imag = right
     tall = jnp.concatenate(

time: 42 us -> 41.6 us (level)
  Pallas kernels: 41.1 us -> 40.6 us
    pallas_call x1, Pallas kernels: 41.1 us -> 40.6 us  [shards(): pl.pallas_call(functools.partial(kernel, groups, chains), out_shape=pltpu...]
where the time goes in v7:
time: 41.6 us; the launch traced here: 41.3 us
  Pallas kernels  40.6 us (98%)
  local copies, waits for them, and re-layouts  0.63 us (2%)
    pallas_call x1, Pallas kernels, shards(): pl.pallas_call(functools.partial(kernel, groups, chains), out_shape=pltpu...  40.6 us

profile of v7, /device:TPU:0, one launch (start us, length us, event | category | flops | bytes accessed | tf_op | source)
XLA Modules:
  0.0 41.3 jit_solution(12456911035960231089)
XLA Ops:
  0.0 40.6 %shard_map.37 = f32[2,8,8,128]{3,2,1,0:T(8,128)S(1)} custom-call(f32[2,128,128]{2,1,0:T(8,128)} %bitcast.5, f32[2,128,128]{2,1,0:T(8,128)} %bitcast.6, s32[8,1,1024]{2,1,0:T(1,128)} %bitcast.7), custom_call_target="tpu_custom_call" | custom-call | tf_op jit(solution)/shard_map/pallas_call | solution.py:503
  40.6 0.6 %copy.6 = f32[2,8,1,1024]{3,2,1,0:T(1,128)} copy(f32[2,8,1,1024]{3,2,1,0:T(1,128)S(1)} %bitcast.4) | data formatting | bytes 131072
